TPU v7x, 32 devices: a whole 2x2x4 slice. The times are simulated.
32 devices in a mesh: region: 2 (over y), tile: 4 (over z), sub: 4 (over x, core).
Axes of the slice: x: 2, y: 2, z: 4, core: 2. Of those that a mesh axis runs over, the one named last changes fastest.
Arguments:
- observations: float32 [8, 65536], P(None, ('region', 'tile', 'sub')), parts along dimension 1, may hold values from -15 to 15
- coords: float32 [2, 65536], P(None, ('region', 'tile')), parts along dimension 1, may hold values from 0 to 71
- pairs: int32 [8, 48, 2], P(('region', 'tile')), parts along dimension 0, may hold values from 0 to 31, as said below
- pair_count: int32 [8], P(('region', 'tile')), parts along dimension 0, may hold values from 15 to 24, as said below
Outputs:
- solution: float32 [8, 65536], P(None, ('region', 'tile', 'sub')), parts along dimension 1
- residual: float32 [8, 65536], P(None, ('region', 'tile', 'sub')), parts along dimension 1
There are 2 independent parts, one for each index of `region`. A program takes and returns all parts, laid end to end along the dimension named above; each array names one. Nothing has to cross between parts.
Inputs may be any that keep to these rules, and one draw needn't show every extreme that they name: In tile-row group g, slots 0 to pair_count[g] - 1 hold distinct pairs (i, j) with g * 8 <= i < (g + 1) * 8 and j one of i, i + 1, i + 2 below 32; every (i, i), and every (i, i + 1) with i + 1 < 32, is among them; the other slots hold (g * 8, g * 8). `pair_count`: some group has 24 live pairs.
All inputs are finite; a program needn't handle non-finite values.
Results may differ from a plain program's by a relative error of at most 0.0059.
The roundings to bfloat16 on the way count: a program that leaves them out, or rounds other values in their place, can miss the bound.
Values may be sent and summed in bfloat16 or wider, within the bound.
A program may use at most 64 MiB of HBM per device.

v0:
```python
import math

import jax
import jax.numpy as jnp
from jax import lax
from jax.sharding import PartitionSpec as P

TS = 1024
ITERS = 2


nugget = 1.0
taper_range = 2.0
matern_range = 4.0
sqrt_three = math.sqrt(3.0)


def shifted(value, axis, by):
    peers = lax.axis_size(axis)
    pairs = [(i, i + by) for i in range(peers) if 0 <= i + by < peers]
    return lax.ppermute(value, axis, pairs)


def covariance_tile(row_coords, col_coords):
    delta_x = row_coords[0][:, None] - col_coords[0][None, :]
    delta_y = row_coords[1][:, None] - col_coords[1][None, :]
    distance = jnp.sqrt(delta_x * delta_x + delta_y * delta_y)
    scaled = sqrt_three * distance / matern_range
    matern = (1.0 + scaled) * jnp.exp(-scaled)
    reach_ratio = distance / taper_range
    falloff = jnp.maximum(1.0 - reach_ratio, 0.0)
    taper_val = falloff * falloff * (1.0 + 0.5 * reach_ratio)
    return (matern * taper_val).astype(jnp.bfloat16)


def local(observations, coords, pairs, pair_count):
    group_id = lax.axis_index("tile")
    members = lax.axis_size("sub")
    member = lax.axis_index("sub")
    block_len = coords.shape[1]
    first_point = group_id * block_len
    next_coords = shifted(coords, "tile", -1)
    window_coords = jnp.concatenate([coords, next_coords], axis=1)
    slot_list = pairs[0]
    live_count = pair_count[0]
    slot_total = slot_list.shape[0]
    usable_slots = slot_total // 2
    share_len = (usable_slots + members - 1) // members
    first_slot = member * share_len
    slot_stride = 1
    turn_count = jnp.maximum(jnp.minimum(first_slot + share_len, live_count) - first_slot, 0)

    def squares(vector):
        return lax.psum(jnp.sum(vector * vector, axis=1), ("tile", "sub"))

    solution = jnp.zeros_like(observations)
    residual = observations
    direction = observations
    norm_now = squares(residual)
    for sweep in range(ITERS):
        rounded = direction.astype(jnp.bfloat16)
        own_block = lax.all_gather(rounded, "sub", axis=1, tiled=True)
        next_block = shifted(own_block, "tile", -1)
        window = jnp.concatenate([own_block, next_block], axis=1)

        def visit_pair(turn_id, totals):
            pair_row = lax.dynamic_index_in_dim(
                slot_list, first_slot + turn_id * slot_stride, 0, keepdims=False
            )
            row_start = pair_row[0] * TS - first_point
            col_start = pair_row[1] * TS - first_point
            cov_tile = covariance_tile(
                lax.dynamic_slice_in_dim(window_coords, row_start, TS, 1),
                lax.dynamic_slice_in_dim(window_coords, col_start, TS, 1),
            )
            row_vec = lax.dynamic_slice_in_dim(window, row_start, TS, 1)
            col_vec = lax.dynamic_slice_in_dim(window, col_start, TS, 1)
            row_part = jnp.dot(col_vec, cov_tile.T, preferred_element_type=jnp.float32)
            col_part = jnp.dot(row_vec, cov_tile, preferred_element_type=jnp.float32)
            cross = jnp.where(pair_row[0] != pair_row[1], 1.0, 0.0).astype(jnp.float32)
            current = lax.dynamic_slice_in_dim(totals, row_start, TS, 1)
            totals = lax.dynamic_update_slice_in_dim(totals, current + row_part, row_start, 1)
            current = lax.dynamic_slice_in_dim(totals, col_start, TS, 1)
            totals = lax.dynamic_update_slice_in_dim(
                totals, current + cross * col_part, col_start, 1
            )
            return totals

        start_totals = jnp.zeros(window.shape, jnp.float32)
        apply_totals = lax.fori_loop(0, turn_count, visit_pair, start_totals)
        carried = shifted(apply_totals[:, block_len:], "tile", 1)
        summed = lax.psum_scatter(
            apply_totals[:, :block_len] + carried, "sub", scatter_dimension=1, tiled=True
        )
        image_vec = nugget * direction + summed
        curvature = lax.psum(jnp.sum(direction * image_vec, axis=1), ("tile", "sub"))
        step_len = norm_now / curvature
        solution = solution + step_len[:, None] * direction
        residual = residual - step_len[:, None] * image_vec
        if sweep + 1 < ITERS:
            norm_next = squares(residual)
        if sweep + 1 < ITERS:
            direction = residual + (norm_next / norm_now)[:, None] * direction
            norm_now = norm_next
    return (solution, residual)


def solution(mesh):
    in_specs = (
        P(None, ("region", "tile", "sub")),
        P(None, ("region", "tile")),
        P(("region", "tile"), None, None),
        P(("region", "tile")),
    )
    out_specs = (P(None, ("region", "tile", "sub")), P(None, ("region", "tile", "sub")))
    return jax.shard_map(local, mesh=mesh, in_specs=in_specs, out_specs=out_specs, check_vma=False)
```

profile of v0, /device:TPU:0, one launch (start us, length us, event | category | flops | bytes accessed | tf_op | source)
XLA Modules:
  0.0 330.8 jit_solution(17218385127048142956)
XLA Ops:
  9.4 6.5 %all_gather.6 = bf16[8,8192]{1,0:T(8,128)(2,1)S(1)} all-gather(bf16[8,2048]{1,0:T(8,128)(2,1)S(1)} %convert_element_type.18), channel_id=1, replica_groups=mesh['region'=2,'tile'=4,'sub'=4] {'sub'}, dimensions={1}, use_global_device_ids=true | all-gather | bytes 163840 | tf_op jit(solution)/shard_map/all_gather | solution.py:62
  18.7 5.7 %collective-permute-done = bf16[8,8192]{1,0:T(8,128)(2,1)S(1)} collective-permute-done((bf16[8,8192]{1,0:T(8,128)(2,1)S(1)}, bf16[8,8192]{1,0:T(8,128)(2,1)S(1)}, u32[]{:S(2)}, u32[]{:S(2)}) %collective-permute-start) | collective-permute-done | bytes 131104 | tf_op jit(solution)/shard_map/ppermute | solution.py:21
  24.4 65.4 %while.24 = (s32[]{:T(128)}, f32[8,16384]{1,0:T(8,128)S(1)}, s32[]{:T(128)}, s32[]{:T(128)}, s32[48,2]{0,1:T(2,128)S(1)}, /*index=5*/s32[]{:T(128)}, bf16[8,1638...) while((s32[]{:T(128)}, f32[8,16384]{1,0:T(8,128)S(1)}, ...), condition=%wide.region_3.4_spmd, body=%wide.region_2.3_spmd.sunk | while | flops 71327760 | bytes 229797 | solution.py:90
  27.7 3.8 %fusion.58 = f32[8,16384]{1,0:T(8,128)S(1)} fusion(f32[8,16384]{1,0:T(8,128)S(1)} %get-tuple-element.410, s32[]{:T(128)S(6)} %select_n.77, f32[1024]{0:T(1024)S(1)} %bitcast.49, f32[1024]{0:T(1024)S(1)} %bitcast.51, f32[1024]{0:T(1024)S(1)} %bitcast.47, f32[1024]{0:T(1024)S(1)} %bitcast.45, bf16[8,16384]{1,0:T(8,128)(2,1)S(1)} %get-tuple-element.431, ...), kind=kOutput, calls=%fused_computation.4.clone.1 | convolution fusion | flops 35659776 | bytes 98312 | tf_op jit(solution)/shard_map/while/body/dot_general | solution.py:78
  31.6 3.8 %fusion.59 = f32[8,16384]{1,0:T(8,128)S(1)} fusion(f32[8,16384]{1,0:T(8,128)S(1)} %fusion.58, s32[]{:T(128)S(6)} %select_n.78, f32[1024]{0:T(1024)S(1)} %bitcast.50, f32[1024]{0:T(1024)S(1)} %bitcast.52, f32[1024]{0:T(1024)S(1)} %bitcast.48, f32[1024]{0:T(1024)S(1)} %bitcast.46, bf16[8,16384]{1,0:T(8,128)(2,1)S(1)} %get-tuple-element.431, ...), kind=kOutput, calls=%fused_computation.7.clone.1 | convolution fusion | flops 35667968 | bytes 98316 | tf_op jit(solution)/shard_map/while/body/dot_general | solution.py:79
  38.6 3.8 %fusion.58 = f32[8,16384]{1,0:T(8,128)S(1)} fusion(f32[8,16384]{1,0:T(8,128)S(1)} %get-tuple-element.410, s32[]{:T(128)S(6)} %select_n.77, f32[1024]{0:T(1024)S(1)} %bitcast.49, f32[1024]{0:T(1024)S(1)} %bitcast.51, f32[1024]{0:T(1024)S(1)} %bitcast.47, f32[1024]{0:T(1024)S(1)} %bitcast.45, bf16[8,16384]{1,0:T(8,128)(2,1)S(1)} %get-tuple-element.431, ...), kind=kOutput, calls=%fused_computation.4.clone.1 | convolution fusion | flops 35659776 | bytes 98312 | tf_op jit(solution)/shard_map/while/body/dot_general | solution.py:78
  42.5 3.8 %fusion.59 = f32[8,16384]{1,0:T(8,128)S(1)} fusion(f32[8,16384]{1,0:T(8,128)S(1)} %fusion.58, s32[]{:T(128)S(6)} %select_n.78, f32[1024]{0:T(1024)S(1)} %bitcast.50, f32[1024]{0:T(1024)S(1)} %bitcast.52, f32[1024]{0:T(1024)S(1)} %bitcast.48, f32[1024]{0:T(1024)S(1)} %bitcast.46, bf16[8,16384]{1,0:T(8,128)(2,1)S(1)} %get-tuple-element.431, ...), kind=kOutput, calls=%fused_computation.7.clone.1 | convolution fusion | flops 35667968 | bytes 98316 | tf_op jit(solution)/shard_map/while/body/dot_general | solution.py:79
  49.5 3.8 %fusion.58 = f32[8,16384]{1,0:T(8,128)S(1)} fusion(f32[8,16384]{1,0:T(8,128)S(1)} %get-tuple-element.410, s32[]{:T(128)S(6)} %select_n.77, f32[1024]{0:T(1024)S(1)} %bitcast.49, f32[1024]{0:T(1024)S(1)} %bitcast.51, f32[1024]{0:T(1024)S(1)} %bitcast.47, f32[1024]{0:T(1024)S(1)} %bitcast.45, bf16[8,16384]{1,0:T(8,128)(2,1)S(1)} %get-tuple-element.431, ...), kind=kOutput, calls=%fused_computation.4.clone.1 | convolution fusion | flops 35659776 | bytes 98312 | tf_op jit(solution)/shard_map/while/body/dot_general | solution.py:78
  53.4 3.8 %fusion.59 = f32[8,16384]{1,0:T(8,128)S(1)} fusion(f32[8,16384]{1,0:T(8,128)S(1)} %fusion.58, s32[]{:T(128)S(6)} %select_n.78, f32[1024]{0:T(1024)S(1)} %bitcast.50, f32[1024]{0:T(1024)S(1)} %bitcast.52, f32[1024]{0:T(1024)S(1)} %bitcast.48, f32[1024]{0:T(1024)S(1)} %bitcast.46, bf16[8,16384]{1,0:T(8,128)(2,1)S(1)} %get-tuple-element.431, ...), kind=kOutput, calls=%fused_computation.7.clone.1 | convolution fusion | flops 35667968 | bytes 98316 | tf_op jit(solution)/shard_map/while/body/dot_general | solution.py:79
  60.4 3.8 %fusion.58 = f32[8,16384]{1,0:T(8,128)S(1)} fusion(f32[8,16384]{1,0:T(8,128)S(1)} %get-tuple-element.410, s32[]{:T(128)S(6)} %select_n.77, f32[1024]{0:T(1024)S(1)} %bitcast.49, f32[1024]{0:T(1024)S(1)} %bitcast.51, f32[1024]{0:T(1024)S(1)} %bitcast.47, f32[1024]{0:T(1024)S(1)} %bitcast.45, bf16[8,16384]{1,0:T(8,128)(2,1)S(1)} %get-tuple-element.431, ...), kind=kOutput, calls=%fused_computation.4.clone.1 | convolution fusion | flops 35659776 | bytes 98312 | tf_op jit(solution)/shard_map/while/body/dot_general | solution.py:78
  64.2 3.8 %fusion.59 = f32[8,16384]{1,0:T(8,128)S(1)} fusion(f32[8,16384]{1,0:T(8,128)S(1)} %fusion.58, s32[]{:T(128)S(6)} %select_n.78, f32[1024]{0:T(1024)S(1)} %bitcast.50, f32[1024]{0:T(1024)S(1)} %bitcast.52, f32[1024]{0:T(1024)S(1)} %bitcast.48, f32[1024]{0:T(1024)S(1)} %bitcast.46, bf16[8,16384]{1,0:T(8,128)(2,1)S(1)} %get-tuple-element.431, ...), kind=kOutput, calls=%fused_computation.7.clone.1 | convolution fusion | flops 35667968 | bytes 98316 | tf_op jit(solution)/shard_map/while/body/dot_general | solution.py:79
  71.3 3.8 %fusion.58 = f32[8,16384]{1,0:T(8,128)S(1)} fusion(f32[8,16384]{1,0:T(8,128)S(1)} %get-tuple-element.410, s32[]{:T(128)S(6)} %select_n.77, f32[1024]{0:T(1024)S(1)} %bitcast.49, f32[1024]{0:T(1024)S(1)} %bitcast.51, f32[1024]{0:T(1024)S(1)} %bitcast.47, f32[1024]{0:T(1024)S(1)} %bitcast.45, bf16[8,16384]{1,0:T(8,128)(2,1)S(1)} %get-tuple-element.431, ...), kind=kOutput, calls=%fused_computation.4.clone.1 | convolution fusion | flops 35659776 | bytes 98312 | tf_op jit(solution)/shard_map/while/body/dot_general | solution.py:78
  75.1 3.8 %fusion.59 = f32[8,16384]{1,0:T(8,128)S(1)} fusion(f32[8,16384]{1,0:T(8,128)S(1)} %fusion.58, s32[]{:T(128)S(6)} %select_n.78, f32[1024]{0:T(1024)S(1)} %bitcast.50, f32[1024]{0:T(1024)S(1)} %bitcast.52, f32[1024]{0:T(1024)S(1)} %bitcast.48, f32[1024]{0:T(1024)S(1)} %bitcast.46, bf16[8,16384]{1,0:T(8,128)(2,1)S(1)} %get-tuple-element.431, ...), kind=kOutput, calls=%fused_computation.7.clone.1 | convolution fusion | flops 35667968 | bytes 98316 | tf_op jit(solution)/shard_map/while/body/dot_general | solution.py:79
  82.2 3.8 %fusion.58 = f32[8,16384]{1,0:T(8,128)S(1)} fusion(f32[8,16384]{1,0:T(8,128)S(1)} %get-tuple-element.410, s32[]{:T(128)S(6)} %select_n.77, f32[1024]{0:T(1024)S(1)} %bitcast.49, f32[1024]{0:T(1024)S(1)} %bitcast.51, f32[1024]{0:T(1024)S(1)} %bitcast.47, f32[1024]{0:T(1024)S(1)} %bitcast.45, bf16[8,16384]{1,0:T(8,128)(2,1)S(1)} %get-tuple-element.431, ...), kind=kOutput, calls=%fused_computation.4.clone.1 | convolution fusion | flops 35659776 | bytes 98312 | tf_op jit(solution)/shard_map/while/body/dot_general | solution.py:78
  86.0 3.8 %fusion.59 = f32[8,16384]{1,0:T(8,128)S(1)} fusion(f32[8,16384]{1,0:T(8,128)S(1)} %fusion.58, s32[]{:T(128)S(6)} %select_n.78, f32[1024]{0:T(1024)S(1)} %bitcast.50, f32[1024]{0:T(1024)S(1)} %bitcast.52, f32[1024]{0:T(1024)S(1)} %bitcast.48, f32[1024]{0:T(1024)S(1)} %bitcast.46, bf16[8,16384]{1,0:T(8,128)(2,1)S(1)} %get-tuple-element.431, ...), kind=kOutput, calls=%fused_computation.7.clone.1 | convolution fusion | flops 35667968 | bytes 98316 | tf_op jit(solution)/shard_map/while/body/dot_general | solution.py:79
  89.9 4.0 %collective-permute-start.2 = (f32[8,8192]{1,0:T(8,128)S(1)}, f32[8,8192]{1,0:T(8,128)S(1)}, u32[]{:S(2)}, u32[]{:S(2)}) collective-permute-start(f32[8,8192]{1,0:T(8,128)S(1)} %slice.93), channel_id=1, source_target_pairs={{0,4},{4,8},{8,12},{1,5},{5,9},{9,13},{2,6},{6,10},{10,14},{3,7},{... | collective-permute-start | bytes 786440 | tf_op jit(solution)/shard_map/ppermute | solution.py:21
  93.9 5.5 %collective-permute-done.2 = f32[8,8192]{1,0:T(8,128)S(1)} collective-permute-done((f32[8,8192]{1,0:T(8,128)S(1)}, f32[8,8192]{1,0:T(8,128)S(1)}, u32[]{:S(2)}, u32[]{:S(2)}) %collective-permute-start.2) | collective-permute-done | bytes 262176 | tf_op jit(solution)/shard_map/ppermute | solution.py:21
  100.2 21.2 %reduce-scatter.3.cloned.1.call-done = f32[8,2048]{1,0:T(8,128)} async-done(((f32[8,8192]{1,0:T(8,128)}), f32[8,2048]{1,0:T(8,128)}) %reduce-scatter.3.cloned.1.call-update) | async-done | bytes 65552 | tf_op jit(solution)/shard_map/reduce_scatter | solution.py:92
  122.4 32.2 %all-reduce = (f32[8]{0:T(128)S(1)}, f32[8]{0:T(128)S(1)}) all-reduce(f32[8]{0:T(128)S(1)} %get-tuple-element.215, f32[8]{0:T(128)S(1)} %get-tuple-element.214), channel_id=1, replica_groups=mesh['region'=2,'tile'=4,'sub'=4] {'tile','sub'}, use_global_device_ids=true, to_apply=%region_1.0 | all-reduce | flops 16 | bytes 128 | tf_op jit(solution)/shard_map/psum | solution.py:54
  154.8 29.5 %psum.30 = f32[8]{0:T(128)S(1)} all-reduce(f32[8]{0:T(128)S(1)} %multiply_reduce_fusion.1), channel_id=1, replica_groups=mesh['region'=2,'tile'=4,'sub'=4] {'tile','sub'}, use_global_device_ids=true, to_apply=%region_8.9 | all-reduce | flops 8 | bytes 64 | tf_op jit(solution)/shard_map/psum | solution.py:54
  184.4 5.4 %all_gather.7 = bf16[8,8192]{1,0:T(8,128)(2,1)S(1)} all-gather(bf16[8,2048]{1,0:T(8,128)(2,1)S(1)} %get-tuple-element.252), channel_id=1, replica_groups=mesh['region'=2,'tile'=4,'sub'=4] {'sub'}, dimensions={1}, use_global_device_ids=true | all-gather | bytes 163840 | tf_op jit(solution)/shard_map/all_gather | solution.py:62
  191.1 6.3 %collective-permute-done.3 = bf16[8,8192]{1,0:T(8,128)(2,1)S(1)} collective-permute-done((bf16[8,8192]{1,0:T(8,128)(2,1)S(1)}, bf16[8,8192]{1,0:T(8,128)(2,1)S(1)}, u32[]{:S(2)}, u32[]{:S(2)}) %collective-permute-start.3) | collective-permute-done | bytes 131104 | tf_op jit(solution)/shard_map/ppermute | solution.py:21
  197.5 65.6 %while.25 = (s32[]{:T(128)}, f32[8,16384]{1,0:T(8,128)S(1)}, s32[]{:T(128)}, s32[]{:T(128)}, s32[48,2]{0,1:T(2,128)S(1)}, /*index=5*/s32[]{:T(128)}, bf16[8,1638...) while((s32[]{:T(128)}, f32[8,16384]{1,0:T(8,128)S(1)}, ...), condition=%wide.region_10.11_spmd, body=%wide.region_9.10_spmd.sunk | while | flops 71327760 | bytes 229797 | solution.py:90
  201.0 3.8 %fusion.63 = f32[8,16384]{1,0:T(8,128)S(1)} fusion(f32[8,16384]{1,0:T(8,128)S(1)} %get-tuple-element.458, s32[]{:T(128)S(6)} %select_n.81, f32[1024]{0:T(1024)S(1)} %bitcast.57, f32[1024]{0:T(1024)S(1)} %bitcast.59, f32[1024]{0:T(1024)S(1)} %bitcast.55, f32[1024]{0:T(1024)S(1)} %bitcast.53, bf16[8,16384]{1,0:T(8,128)(2,1)S(1)} %get-tuple-element.479, ...), kind=kOutput, calls=%fused_computation.29.clone.1 | convolution fusion | flops 35659776 | bytes 98312 | tf_op jit(solution)/shard_map/while/body/dot_general | solution.py:78
  211.9 3.8 %fusion.63 = f32[8,16384]{1,0:T(8,128)S(1)} fusion(f32[8,16384]{1,0:T(8,128)S(1)} %get-tuple-element.458, s32[]{:T(128)S(6)} %select_n.81, f32[1024]{0:T(1024)S(1)} %bitcast.57, f32[1024]{0:T(1024)S(1)} %bitcast.59, f32[1024]{0:T(1024)S(1)} %bitcast.55, f32[1024]{0:T(1024)S(1)} %bitcast.53, bf16[8,16384]{1,0:T(8,128)(2,1)S(1)} %get-tuple-element.479, ...), kind=kOutput, calls=%fused_computation.29.clone.1 | convolution fusion | flops 35659776 | bytes 98312 | tf_op jit(solution)/shard_map/while/body/dot_general | solution.py:78
  222.8 3.8 %fusion.63 = f32[8,16384]{1,0:T(8,128)S(1)} fusion(f32[8,16384]{1,0:T(8,128)S(1)} %get-tuple-element.458, s32[]{:T(128)S(6)} %select_n.81, f32[1024]{0:T(1024)S(1)} %bitcast.57, f32[1024]{0:T(1024)S(1)} %bitcast.59, f32[1024]{0:T(1024)S(1)} %bitcast.55, f32[1024]{0:T(1024)S(1)} %bitcast.53, bf16[8,16384]{1,0:T(8,128)(2,1)S(1)} %get-tuple-element.479, ...), kind=kOutput, calls=%fused_computation.29.clone.1 | convolution fusion | flops 35659776 | bytes 98312 | tf_op jit(solution)/shard_map/while/body/dot_general | solution.py:78
  233.6 3.8 %fusion.63 = f32[8,16384]{1,0:T(8,128)S(1)} fusion(f32[8,16384]{1,0:T(8,128)S(1)} %get-tuple-element.458, s32[]{:T(128)S(6)} %select_n.81, f32[1024]{0:T(1024)S(1)} %bitcast.57, f32[1024]{0:T(1024)S(1)} %bitcast.59, f32[1024]{0:T(1024)S(1)} %bitcast.55, f32[1024]{0:T(1024)S(1)} %bitcast.53, bf16[8,16384]{1,0:T(8,128)(2,1)S(1)} %get-tuple-element.479, ...), kind=kOutput, calls=%fused_computation.29.clone.1 | convolution fusion | flops 35659776 | bytes 98312 | tf_op jit(solution)/shard_map/while/body/dot_general | solution.py:78
  244.5 3.8 %fusion.63 = f32[8,16384]{1,0:T(8,128)S(1)} fusion(f32[8,16384]{1,0:T(8,128)S(1)} %get-tuple-element.458, s32[]{:T(128)S(6)} %select_n.81, f32[1024]{0:T(1024)S(1)} %bitcast.57, f32[1024]{0:T(1024)S(1)} %bitcast.59, f32[1024]{0:T(1024)S(1)} %bitcast.55, f32[1024]{0:T(1024)S(1)} %bitcast.53, bf16[8,16384]{1,0:T(8,128)(2,1)S(1)} %get-tuple-element.479, ...), kind=kOutput, calls=%fused_computation.29.clone.1 | convolution fusion | flops 35659776 | bytes 98312 | tf_op jit(solution)/shard_map/while/body/dot_general | solution.py:78
  255.4 3.8 %fusion.63 = f32[8,16384]{1,0:T(8,128)S(1)} fusion(f32[8,16384]{1,0:T(8,128)S(1)} %get-tuple-element.458, s32[]{:T(128)S(6)} %select_n.81, f32[1024]{0:T(1024)S(1)} %bitcast.57, f32[1024]{0:T(1024)S(1)} %bitcast.59, f32[1024]{0:T(1024)S(1)} %bitcast.55, f32[1024]{0:T(1024)S(1)} %bitcast.53, bf16[8,16384]{1,0:T(8,128)(2,1)S(1)} %get-tuple-element.479, ...), kind=kOutput, calls=%fused_computation.29.clone.1 | convolution fusion | flops 35659776 | bytes 98312 | tf_op jit(solution)/shard_map/while/body/dot_general | solution.py:78
  264.5 5.4 %collective-permute-done.4 = f32[8,8192]{1,0:T(8,128)S(1)} collective-permute-done((f32[8,8192]{1,0:T(8,128)S(1)}, f32[8,8192]{1,0:T(8,128)S(1)}, u32[]{:S(2)}, u32[]{:S(2)}) %collective-permute-start.4) | collective-permute-done | bytes 262176 | tf_op jit(solution)/shard_map/ppermute | solution.py:21
  270.6 19.4 %reduce-scatter.5.cloned.1.call-done = f32[8,2048]{1,0:T(8,128)} async-done(((f32[8,8192]{1,0:T(8,128)}), f32[8,2048]{1,0:T(8,128)}) %reduce-scatter.5.cloned.1.call-update) | async-done | bytes 65552 | tf_op jit(solution)/shard_map/reduce_scatter | solution.py:92
  291.0 32.2 %psum.31 = f32[8]{0:T(128)S(1)} all-reduce(f32[8]{0:T(128)S(1)} %get-tuple-element.250), channel_id=1, replica_groups=mesh['region'=2,'tile'=4,'sub'=4] {'tile','sub'}, use_global_device_ids=true, to_apply=%region_13.14 | all-reduce | flops 8 | bytes 64 | tf_op jit(solution)/shard_map/psum | solution.py:96
  (74 shorter events, 43.7 us)
Async XLA Ops:
  7.2 114.2 %reduce-scatter.3.cloned.1.call-start = ((), (), s32[]{:S(2)}) async-start(), calls=%async_computation.2 | async-start | bytes 327680 | tf_op jit(solution)/shard_map/reduce_scatter | solution.py:92
  7.2 11.4 %collective-permute-start.1 = (f32[2,8192]{1,0:T(2,128)}, f32[2,8192]{1,0:T(2,128)S(1)}, u32[]{:S(2)}, u32[]{:S(2)}) collective-permute-start(f32[2,8192]{1,0:T(2,128)} %param.9), channel_id=1, source_target_pairs={{4,0},{8,4},{12,8},{5,1},{9,5},{13,9},{6,2},{10,6},{14,10},{7,3},{... | collective-permute-start | bytes 196616 | tf_op jit(solution)/shard_map/ppermute | solution.py:21
  15.8 8.5 %collective-permute-start = (bf16[8,8192]{1,0:T(8,128)(2,1)S(1)}, bf16[8,8192]{1,0:T(8,128)(2,1)S(1)}, u32[]{:S(2)}, u32[]{:S(2)}) collective-permute-start(bf16[8,8192]{1,0:T(8,128)(2,1)S(1)} %all_gather.6), channel_id=1, source_target_pairs={{4,0},{8,4},{12,8},{5,1},{9,5},{13,9},{6,2},{10,6},{14,10},{7,3},{... | collective-permute-start | bytes 393224 | tf_op jit(solution)/shard_map/ppermute | solution.py:21
  18.6 5.8 %copy-start.1 = (s32[1,48,2]{1,2,0:T(2,128)S(1)}, s32[1,48,2]{1,2,0:T(2,128)}, u32[]{:S(2)}) copy-start(s32[1,48,2]{1,2,0:T(2,128)} %param.10) | copy-start | bytes 1156
  89.8 31.5 %copy-start = (f32[8,2048]{1,0:T(8,128)S(1)}, f32[8,2048]{1,0:T(8,128)}, u32[]{:S(2)}) copy-start(f32[8,2048]{1,0:T(8,128)} %param.8) | copy-start | bytes 196612
  89.9 9.5 %collective-permute-start.2 = (f32[8,8192]{1,0:T(8,128)S(1)}, f32[8,8192]{1,0:T(8,128)S(1)}, u32[]{:S(2)}, u32[]{:S(2)}) collective-permute-start(f32[8,8192]{1,0:T(8,128)S(1)} %slice.93), channel_id=1, source_target_pairs={{0,4},{4,8},{8,12},{1,5},{5,9},{9,13},{2,6},{6,10},{10,14},{3,7},{... | collective-permute-start | bytes 786440 | tf_op jit(solution)/shard_map/ppermute | solution.py:21
  100.1 189.9 %reduce-scatter.5.cloned.1.call-start = ((), (), s32[]{:S(2)}) async-start(), calls=%async_computation.3 | async-start | bytes 327680 | tf_op jit(solution)/shard_map/reduce_scatter | solution.py:92
  189.8 7.6 %collective-permute-start.3 = (bf16[8,8192]{1,0:T(8,128)(2,1)S(1)}, bf16[8,8192]{1,0:T(8,128)(2,1)S(1)}, u32[]{:S(2)}, u32[]{:S(2)}) collective-permute-start(bf16[8,8192]{1,0:T(8,128)(2,1)S(1)} %all_gather.7), channel_id=1, source_target_pairs={{4,0},{8,4},{12,8},{5,1},{9,5},{13,9},{6,2},{10,6},{14,10},{7,3},{... | collective-permute-start | bytes 393224 | tf_op jit(solution)/shard_map/ppermute | solution.py:21
  263.1 6.8 %collective-permute-start.4 = (f32[8,8192]{1,0:T(8,128)S(1)}, f32[8,8192]{1,0:T(8,128)S(1)}, u32[]{:S(2)}, u32[]{:S(2)}) collective-permute-start(f32[8,8192]{1,0:T(8,128)S(1)} %slice.95), channel_id=1, source_target_pairs={{0,4},{4,8},{8,12},{1,5},{5,9},{9,13},{2,6},{6,10},{10,14},{3,7},{... | collective-permute-start | bytes 786440 | tf_op jit(solution)/shard_map/ppermute | solution.py:21
Sparse Core Ops, SparseCore 0:
  100.3 21.0 reduce-scatter.2
  270.8 19.1 reduce-scatter.4
where the time goes:
time: 331 us
  blocking collectives  106 us (32%)
  matrix products  91.3 us (28%)
  waiting for transfers between devices  63.5 us (19%)
  loops' own time  30.5 us (9%)
  between operations  14.8 us (4%)
  local copies, waits for them, and re-layouts  10.2 us (3%)
  starting transfers between devices  9.41 us (3%)
  other arithmetic  5.37 us (2%)
    psum x2, blocking collectives, squares(): return lax.psum(jnp.sum(vector * vector, axis=1), ('tile', 'sub'))  61.7 us
    dot_general x12, matrix products, visit_pair(): row_part = jnp.dot(col_vec, cov_tile.T, preferred_element_type=jnp.float32)  45.8 us
    dot_general x12, matrix products, visit_pair(): col_part = jnp.dot(row_vec, cov_tile, preferred_element_type=jnp.float32)  45.5 us
    reduce_scatter x2, waiting for transfers between devices, local(): lax.psum_scatter(apply_totals[:, :block_len] + carried, 'sub', scatter_di...  40.5 us
    psum x1, blocking collectives, local(): lax.psum(jnp.sum(direction * image_vec, axis=1), ('tile', 'sub'))  32.2 us
    another operation x2, loops' own time, local(): apply_totals = lax.fori_loop(0, turn_count, visit_pair, start_totals)  30.5 us
    ppermute x5, waiting for transfers between devices, shifted(): return lax.ppermute(value, axis, pairs)  22.9 us
    all_gather x2, blocking collectives, local(): own_block = lax.all_gather(rounded, 'sub', axis=1, tiled=True)  11.9 us
  transfers between devices with their start and end apart: 7, of which 6 were waited for; matrix products, arithmetic and copies ran while one was open for 1% of the time, Pallas kernels for 0%

commit v1 on v0

v1 whole, which is shorter than its diff:
```python
import functools
import math

import jax
import jax.numpy as jnp
from jax import lax
from jax.experimental import pallas as pl
from jax.experimental.pallas import tpu as pltpu
from jax.sharding import PartitionSpec as P

TS = 1024
PIECE = 256
STEPS = TS // PIECE
MESH = pl.DeviceIdType.MESH

LN2 = math.log(2.0)
SCALE = math.sqrt(3.0) / 4.0 / LN2
EDGE = 2.0 * SCALE
FOLD = 2.0**-EDGE / EDGE**2
B0 = 1.5 * (1.0 + EDGE * LN2) * FOLD
B1 = -(1.5 * LN2 + (1.0 + EDGE * LN2) / (2.0 * EDGE)) * FOLD
B2 = LN2 / (2.0 * EDGE) * FOLD


def covariance(xr, yr, xc, yc):
    dx = xr - xc
    dy = yr - yc
    square = jnp.maximum(dx * dx + dy * dy, 1e-30)
    w = jnp.maximum(EDGE - square * lax.rsqrt(square), 0.0)
    poly = (B2 * w + B1) * w + B0
    return ((w * w) * poly * jnp.exp2(w)).astype(jnp.bfloat16)


def kernel(nt, ns, tiles, obs, coords, pairs, count, x_out, r_out,
           win_c, row_c, win_r, win_q, vb, tot1, tot2, got1, got2, diag_c, full_c,
           part, sub1, tile1, sub2, tile2, mid, send_sem, recv_sem):
    own = tiles * TS
    nd = nt * ns
    tile_id = lax.axis_index("tile")
    sub_id = lax.axis_index("sub")
    me = tile_id * ns + sub_id
    halo = [(h, h // tiles, h % tiles) for h in (tiles, tiles + 1)]
    reach = (tiles + 1) // tiles

    def linear(offset):
        d = lax.rem(me + offset + nd, nd)
        return {"tile": lax.div(d, ns), "sub": lax.rem(d, ns)}

    def sub_peer(offset):
        return {"sub": lax.rem(sub_id + offset, ns)}

    def tile_peer(offset):
        return {"tile": lax.rem(tile_id + offset, nt)}

    barrier = pltpu.get_barrier_semaphore()
    greet = [linear(k) for k in range(1, reach + 1)] + [linear(-k) for k in range(1, reach + 1)]
    greet += [sub_peer(d) for d in range(1, ns)] + [tile_peer(d) for d in range(1, nt)]
    for device in greet:
        pl.semaphore_signal(barrier, inc=1, device_id=device, device_id_type=MESH)

    used = [0]

    def send(src, dst, device):
        at = used[0]
        used[0] += 1
        copy = pltpu.make_async_remote_copy(
            src_ref=src, dst_ref=dst, send_sem=send_sem.at[at], recv_sem=recv_sem.at[at],
            device_id=device, device_id_type=MESH)
        copy.start()
        return copy

    def tile_of(ref, t):
        return ref.at[:, t * TS:(t + 1) * TS]

    first = pl.multiple_of(sub_id * own, own)
    mine = coords[:, pl.ds(first, own)] * SCALE
    win_c[:, 0:own] = mine
    win_r[:, 0:own] = obs[...]
    row_c[...] = jnp.transpose(jnp.concatenate([mine] * 4, axis=0))
    vb[0:8, 0:own] = obs[...].astype(jnp.bfloat16)
    vb[8:16, :] = jnp.zeros((8, own + 2 * TS), jnp.bfloat16)
    tot1[...] = jnp.zeros_like(tot1)
    tot2[...] = jnp.zeros_like(tot2)

    slot = lax.broadcasted_iota(jnp.int32, (pairs.shape[0], 1), 0)
    alive = slot < count[0]
    pi, pj = pairs[:, 0:1], pairs[:, 1:2]

    def far_flag(o):
        i = me * tiles + o
        hit = (pi == i) & (pj == i + 2) & alive
        return jnp.max(jnp.where(hit, 1.0, 0.0), axis=0, keepdims=True)

    def near_flag(o):
        return jnp.where(me * tiles + o + 1 < nd * tiles, 1.0, 0.0).astype(jnp.float32)

    pl.semaphore_wait(barrier, len(greet))
    sent = []
    wait_c = [send(tile_of(win_c, o), tile_of(win_c, h), linear(-k)) for h, k, o in halo]
    wait_r = [send(tile_of(win_r, o), tile_of(win_r, h), linear(-k)) for h, k, o in halo]
    sent += wait_c + wait_r

    def fold(value):
        return value[0:8] + value[8:16]

    def contract(tot, o, h, rows, chunk, flag):
        at = pl.multiple_of(o * TS + rows, PIECE)
        here = vb[:, pl.ds(at, PIECE)]
        there = vb[:, h * TS:(h + 1) * TS]
        col = fold(jnp.dot(here, chunk, preferred_element_type=jnp.float32))
        row = fold(lax.dot_general(there, chunk, (((1,), (1,)), ((), ())),
                                   preferred_element_type=jnp.float32))
        if flag is not None:
            col, row = col * flag, row * flag
        tot[:, h * TS:(h + 1) * TS] += col
        tot[:, pl.ds(at, PIECE)] += row

    def cov_chunk(o, h, rows):
        at = pl.multiple_of(o * TS + rows, PIECE)
        xr, yr = row_c[pl.ds(at, PIECE), 0:1], row_c[pl.ds(at, PIECE), 1:2]
        xc, yc = win_c[0:1, h * TS:(h + 1) * TS], win_c[1:2, h * TS:(h + 1) * TS]
        return covariance(xr, yr, xc, yc)

    blocks = [(o, o + 1) for o in range(tiles)] + [(o, o + 2) for o in range(tiles)]
    local = [b for b, (o, h) in enumerate(blocks) if h < tiles]
    cross = [b for b, (o, h) in enumerate(blocks) if h >= tiles]
    flags = {}
    for b, (o, h) in enumerate(blocks):
        if h - o == 2:
            flags[b] = far_flag(o)
        else:
            flags[b] = near_flag(o) if h >= tiles else None

    def full_block(b, tot, build):
        o, h = blocks[b]

        def step(i, carry):
            rows = pl.multiple_of(i * PIECE, PIECE)
            if build:
                chunk = cov_chunk(o, h, rows)
                full_c[b, pl.ds(rows, PIECE), :] = chunk
            else:
                chunk = full_c[b, pl.ds(rows, PIECE), :]
            contract(tot, o, h, rows, chunk, flags[b])
            return carry

        lax.fori_loop(0, STEPS, step, 0)

    def diag_block(o, tot, build):
        for k in range(STEPS):
            for l in range(k, STEPS):
                rk = slice(o * TS + k * PIECE, o * TS + (k + 1) * PIECE)
                rl = slice(o * TS + l * PIECE, o * TS + (l + 1) * PIECE)
                ck, cl = slice(k * PIECE, (k + 1) * PIECE), slice(l * PIECE, (l + 1) * PIECE)
                if build:
                    chunk = covariance(row_c[rk, 0:1], row_c[rk, 1:2], win_c[0:1, rl], win_c[1:2, rl])
                    diag_c[o, ck, cl] = chunk
                else:
                    chunk = diag_c[o, ck, cl]
                tot[:, rl] += fold(jnp.dot(vb[:, rk], chunk, preferred_element_type=jnp.float32))
                if k != l:
                    tot[:, rk] += fold(lax.dot_general(
                        vb[:, rl], chunk, (((1,), (1,)), ((), ())), preferred_element_type=jnp.float32))

    def spread(partial, dst, peer, n):
        return [send(partial, dst.at[d - 1], peer(d)) for d in range(1, n)]

    def gathered(own_part, copies, dst):
        total = own_part
        for d, copy in enumerate(copies):
            copy.wait_recv()
            total = total + dst[d]
        return total

    for o in range(tiles - 1):
        diag_block(o, tot1, True)
    for b in local:
        full_block(b, tot1, True)
    for copy in wait_c + wait_r:
        copy.wait_recv()
    vb[0:8, own:] = win_r[:, own:].astype(jnp.bfloat16)
    for b in cross:
        full_block(b, tot1, True)
    wait_1 = [send(tile_of(tot1, h), got1.at[h - tiles], linear(k)) for h, k, o in halo]
    sent += wait_1
    diag_block(tiles - 1, tot1, True)
    for copy in wait_1:
        copy.wait_recv()

    r0 = win_r[:, 0:own]
    win_q[:, 0:own] = r0 + tot1[:, 0:own]
    for h, k, o in halo:
        mask = jnp.where(me >= k, 1.0, 0.0).astype(jnp.float32)
        win_q[:, o * TS:(o + 1) * TS] += got1[h - tiles] * mask
    wait_q = [send(tile_of(win_q, o), tile_of(win_q, h), linear(-k)) for h, k, o in halo]
    sent += wait_q
    q0 = win_q[:, 0:own]
    high = q0.astype(jnp.bfloat16)
    vb[0:8, 0:own] = high
    vb[8:16, 0:own] = (q0 - high.astype(jnp.float32)).astype(jnp.bfloat16)

    lane = lax.broadcasted_iota(jnp.int32, (8, 128), 1)
    rr = jnp.sum(r0 * r0, axis=1, keepdims=True)
    rq = jnp.sum(r0 * q0, axis=1, keepdims=True)
    qq = jnp.sum(q0 * q0, axis=1, keepdims=True)
    part[0] = jnp.where(lane == 0, rr, jnp.where(lane == 1, rq, qq))
    go_sub = spread(part.at[0], sub1, sub_peer, ns)
    sent += go_sub

    for o in range(tiles - 1):
        diag_block(o, tot2, False)
    for b in local:
        full_block(b, tot2, False)
    part[1] = gathered(part[0], go_sub, sub1)
    go_tile = spread(part.at[1], tile1, tile_peer, nt)
    sent += go_tile
    for copy in wait_q:
        copy.wait_recv()
    far_q = win_q[:, own:]
    high = far_q.astype(jnp.bfloat16)
    vb[0:8, own:] = high
    vb[8:16, own:] = (far_q - high.astype(jnp.float32)).astype(jnp.bfloat16)
    for b in cross:
        full_block(b, tot2, False)
    wait_2 = [send(tile_of(tot2, h), got2.at[h - tiles], linear(k)) for h, k, o in halo]
    sent += wait_2
    diag_block(tiles - 1, tot2, False)

    sums = gathered(part[1], go_tile, tile1)
    rr, rq, qq = sums[:, 0:1], sums[:, 1:2], sums[:, 2:3]
    alpha = rr / rq
    new = alpha * alpha * qq - rr
    beta = new / rr
    near = 1.0 + beta

    d_win = near * win_r[...] - alpha * win_q[...]
    t_win = near * tot1[...] - alpha * tot2[...]
    d_own = d_win[:, 0:own]
    bend = jnp.sum(d_win * t_win, axis=1, keepdims=True) + jnp.sum(d_own * d_own, axis=1, keepdims=True)
    part[2] = jnp.broadcast_to(bend, (8, 128))
    go_sub = spread(part.at[2], sub2, sub_peer, ns)
    sent += go_sub
    part[3] = gathered(part[2], go_sub, sub2)
    go_tile = spread(part.at[3], tile2, tile_peer, nt)
    sent += go_tile

    for copy in wait_2:
        copy.wait_recv()
    r0 = win_r[:, 0:own]
    q0 = win_q[:, 0:own]
    mid[0] = q0 + tot2[:, 0:own]
    for h, k, o in halo:
        mask = jnp.where(me >= k, 1.0, 0.0).astype(jnp.float32)
        mid[0, :, o * TS:(o + 1) * TS] += got2[h - tiles] * mask
    mid[0] = near * q0 - alpha * mid[0]
    mid[1] = r0 - alpha * q0
    mid[2] = near * r0 - alpha * q0
    bend = gathered(part[3], go_tile, tile2)[:, 0:1]
    step = new / bend
    x_out[...] = alpha * r0 + step * mid[2]
    r_out[...] = mid[1] - step * mid[0]
    for copy in sent:
        copy.wait_send()


def local(nt, ns, observations, coords, pairs, pair_count):
    own = observations.shape[1]
    tiles = own // TS
    window = own + 2 * TS
    f32 = jnp.float32
    copies = 10 + 2 * (ns - 1) + 2 * (nt - 1)
    out = jax.ShapeDtypeStruct(observations.shape, f32)
    vmem = pl.BlockSpec(memory_space=pltpu.VMEM)
    return pl.pallas_call(
        functools.partial(kernel, nt, ns, tiles),
        out_shape=(out, out),
        in_specs=[vmem, vmem, vmem, pl.BlockSpec(memory_space=pltpu.SMEM)],
        out_specs=(vmem, vmem),
        scratch_shapes=[
            pltpu.VMEM((2, window), f32),
            pltpu.VMEM((own, 8), f32),
            pltpu.VMEM((8, window), f32),
            pltpu.VMEM((8, window), f32),
            pltpu.VMEM((16, window), jnp.bfloat16),
            pltpu.VMEM((8, window), f32),
            pltpu.VMEM((8, window), f32),
            pltpu.VMEM((2, 8, TS), f32),
            pltpu.VMEM((2, 8, TS), f32),
            pltpu.VMEM((tiles, TS, TS), jnp.bfloat16),
            pltpu.VMEM((2 * tiles, TS, TS), jnp.bfloat16),
            pltpu.VMEM((4, 8, 128), f32),
            pltpu.VMEM((ns - 1, 8, 128), f32),
            pltpu.VMEM((nt - 1, 8, 128), f32),
            pltpu.VMEM((ns - 1, 8, 128), f32),
            pltpu.VMEM((nt - 1, 8, 128), f32),
            pltpu.VMEM((3, 8, own), f32),
            pltpu.SemaphoreType.DMA((copies,)),
            pltpu.SemaphoreType.DMA((copies,)),
        ],
        compiler_params=pltpu.CompilerParams(
            collective_id=0, has_side_effects=True, vmem_limit_bytes=48 * 1024 * 1024),
    )(observations, coords, pairs[0], pair_count)


def solution(mesh):
    in_specs = (
        P(None, ("region", "tile", "sub")),
        P(None, ("region", "tile")),
        P(("region", "tile"), None, None),
        P(("region", "tile")),
    )
    out_specs = (P(None, ("region", "tile", "sub")), P(None, ("region", "tile", "sub")))
    body = functools.partial(local, mesh.shape["tile"], mesh.shape["sub"])
    return jax.shard_map(body, mesh=mesh, in_specs=in_specs, out_specs=out_specs, check_vma=False)
```

time: 331 us -> 46.8 us (0.14)
  blocking collectives: 106 us -> 0 us
  matrix products: 91.3 us -> 0 us
  waiting for transfers between devices: 63.5 us -> 0 us
  Pallas kernels: 0 us -> 41.5 us
  loops' own time: 30.5 us -> 0 us
  between operations: 14.8 us -> 1.3 us
  starting transfers between devices: 9.41 us -> 0 us
  local copies, waits for them, and re-layouts: 10.2 us -> 3.7 us
  other arithmetic: 5.37 us -> 0 us
    psum x3 -> x0, blocking collectives: 93.9 us -> none  [the longest x2 61.7 us: squares(): return lax.psum(jnp.sum(vector * vector, axis=1), ('tile', 'sub'))]
    dot_general x24 -> x0, matrix products: 91.3 us -> none  [the longest x12 45.8 us: visit_pair(): row_part = jnp.dot(col_vec, cov_tile.T, preferred_element_type=jnp.float32)]
    pallas_call x0 -> x1, Pallas kernels: none -> 41.5 us  [local(): pl.pallas_call(functools.partial(kernel, nt, ns, tiles), out_shape=(out,...]
    reduce_scatter x2 -> x0, waiting for transfers between devices: 40.5 us -> none  [local(): lax.psum_scatter(apply_totals[:, :block_len] + carried, 'sub', scatter_di...]
    another operation x2 -> x0, loops' own time: 30.5 us -> none  [local(): apply_totals = lax.fori_loop(0, turn_count, visit_pair, start_totals)]
    ppermute x5 -> x0, waiting for transfers between devices: 22.9 us -> none  [shifted(): return lax.ppermute(value, axis, pairs)]
    all_gather x2 -> x0, blocking collectives: 11.9 us -> none  [local(): own_block = lax.all_gather(rounded, 'sub', axis=1, tiled=True)]
    ppermute x5 -> x0, starting transfers between devices: 9.34 us -> none  [shifted(): return lax.ppermute(value, axis, pairs)]
  transfers between devices with their start and end apart: 7 -> 0, of which waited for: 6 -> 0; matrix products, arithmetic and copies ran while one was open for 1% -> 0% of each run, Pallas kernels for 0% -> 0%
where the time goes in v1:
time: 46.8 us; the launch traced here: 46.5 us
  Pallas kernels  41.5 us (89%)
  local copies, waits for them, and re-layouts  3.7 us (8%)
  between operations  1.3 us (3%)
    pallas_call x1, Pallas kernels, local(): pl.pallas_call(functools.partial(kernel, nt, ns, tiles), out_shape=(out,...  41.5 us
    unnamed x8, local copies, waits for them, and re-layouts  3.61 us

profile of v1, /device:TPU:0, one launch (start us, length us, event | category | flops | bytes accessed | tf_op | source)
XLA Modules:
  0.0 46.5 jit_solution(936498072003766547)
XLA Ops:
  1.3 0.0 copy-start.2
  1.3 0.7 %copy-done.2 = s32[1,48,2]{1,2,0:T(2,128)S(1)} copy-done((s32[1,48,2]{1,2,0:T(2,128)S(1)}, s32[1,48,2]{1,2,0:T(2,128)}, u32[]{:S(2)}) %copy-start.2) | copy-done | bytes 408
  2.0 0.1 copy.6.pairs
  2.0 0.0 copy-start
  2.1 0.8 %copy-done = f32[8,2048]{1,0:T(8,128)S(1)} copy-done((f32[8,2048]{1,0:T(8,128)S(1)}, f32[8,2048]{1,0:T(8,128)}, u32[]{:S(2)}) %copy-start) | copy-done | bytes 65560
  2.9 0.0 copy-start.1
  2.9 0.8 %copy-done.1 = f32[2,8192]{1,0:T(2,128)S(1)} copy-done((f32[2,8192]{1,0:T(2,128)S(1)}, f32[2,8192]{1,0:T(2,128)}, u32[]{:S(2)}) %copy-start.1) | copy-done | bytes 65560
  3.7 41.5 %shard_map.59 = (f32[8,2048]{1,0:T(8,128)S(1)}, f32[8,2048]{1,0:T(8,128)S(1)}) custom-call(f32[8,2048]{1,0:T(8,128)S(1)} %copy-done, f32[2,8192]{1,0:T(2,128)S(1)} %copy-done.1, s32[48,2]{1,0:T(8,128)S(1)} %copy.6.pairs, s32[1]{0:T(128)S(6)} %copy.9.count), custom_call_target="tpu_custom_call" | custom-call | tf_op jit(solution)/shard_map/pallas_call | solution.py:274
  45.3 0.6 %copy.10 = f32[8,2048]{1,0:T(8,128)} copy(f32[8,2048]{1,0:T(8,128)S(1)} %get-tuple-element.4) | data formatting | bytes 131072
  45.9 0.6 %copy.11 = f32[8,2048]{1,0:T(8,128)} copy(f32[8,2048]{1,0:T(8,128)S(1)} %get-tuple-element.5) | data formatting | bytes 131072
Async XLA Ops:
  1.3 0.7 %copy-start.2 = (s32[1,48,2]{1,2,0:T(2,128)S(1)}, s32[1,48,2]{1,2,0:T(2,128)}, u32[]{:S(2)}) copy-start(s32[1,48,2]{1,2,0:T(2,128)} %param.6) | copy-start | bytes 1156
  2.0 0.8 %copy-start = (f32[8,2048]{1,0:T(8,128)S(1)}, f32[8,2048]{1,0:T(8,128)}, u32[]{:S(2)}) copy-start(f32[8,2048]{1,0:T(8,128)} %obs.1) | copy-start | bytes 196612
  2.9 0.8 %copy-start.1 = (f32[2,8192]{1,0:T(2,128)S(1)}, f32[2,8192]{1,0:T(2,128)}, u32[]{:S(2)}) copy-start(f32[2,8192]{1,0:T(2,128)} %coords.1) | copy-start | bytes 196612

commit v2 on v1

v2 whole, which is shorter than its diff:
```python
import functools
import math

import jax
import jax.numpy as jnp
from jax import lax
from jax.experimental import pallas as pl
from jax.experimental.pallas import tpu as pltpu
from jax.sharding import PartitionSpec as P

TS = 1024
PIECE = 256
STEPS = TS // PIECE
MESH = pl.DeviceIdType.MESH

LN2 = math.log(2.0)
SCALE = math.sqrt(3.0) / 4.0 / LN2
EDGE = 2.0 * SCALE
FOLD = 2.0**-EDGE / EDGE**2
B0 = 1.5 * (1.0 + EDGE * LN2) * FOLD
B1 = -(1.5 * LN2 + (1.0 + EDGE * LN2) / (2.0 * EDGE)) * FOLD
B2 = LN2 / (2.0 * EDGE) * FOLD


def covariance(xr, yr, xc, yc):
    dx = xr - xc
    dy = yr - yc
    square = jnp.maximum(dx * dx + dy * dy, 1e-30)
    w = jnp.maximum(EDGE - square * lax.rsqrt(square), 0.0)
    poly = (B2 * w + B1) * w + B0
    return ((w * w) * poly * jnp.exp2(w)).astype(jnp.bfloat16)


def kernel(nt, ns, tiles, obs, coords, pairs_in, count_in, x_out, r_out,
           c_in, pairs, count, win_c, row_c, win_r, win_q, vb, tot1, tot2, got1, got2, diag_c, full_c,
           part, gather1, mid, load_sem, send_sem, recv_sem):
    own = tiles * TS
    nd = nt * ns
    tile_id = lax.axis_index("tile")
    sub_id = lax.axis_index("sub")
    me = tile_id * ns + sub_id
    if tiles == 1:
        spans = [(TS, TS, 1, 0), (2 * TS, TS, 2, 0)]
    else:
        spans = [(own, 2 * TS, 1, 0)]
    direct = nd <= 16

    def linear(offset):
        d = lax.rem(me + offset + nd, nd)
        return {"tile": lax.div(d, ns), "sub": lax.rem(d, ns)}

    def sub_peer(offset):
        return {"sub": lax.rem(sub_id + offset, ns)}

    def tile_peer(offset):
        return {"tile": lax.rem(tile_id + offset, nt)}

    win_c[:, own:] = jnp.zeros((2, 2 * TS), jnp.float32)
    win_r[:, own:] = jnp.zeros((8, 2 * TS), jnp.float32)
    win_q[:, own:] = jnp.zeros((8, 2 * TS), jnp.float32)
    barrier = pltpu.get_barrier_semaphore()
    if direct:
        greet = [linear(d) for d in range(1, nd)]
    else:
        greet = [linear(k) for _, _, k, _ in spans] + [linear(-k) for _, _, k, _ in spans]
        greet += [sub_peer(d) for d in range(1, ns)] + [tile_peer(d) for d in range(1, nt)]
    for device in greet:
        pl.semaphore_signal(barrier, inc=1, device_id=device, device_id_type=MESH)

    first = pl.multiple_of(sub_id * own, own)
    loads = [
        pltpu.make_async_copy(coords.at[:, pl.ds(first, own)], c_in, load_sem.at[0]),
        pltpu.make_async_copy(obs, win_r.at[:, 0:own], load_sem.at[1]),
        pltpu.make_async_copy(pairs_in, pairs, load_sem.at[2]),
        pltpu.make_async_copy(count_in, count, load_sem.at[3]),
    ]
    for copy in loads:
        copy.start()

    used = [0]
    sent = []

    def send(src, dst, device, gives=None, takes=None):
        at = used[0]
        used[0] += 1
        copy = pltpu.make_async_remote_copy(
            src_ref=src, dst_ref=dst, send_sem=send_sem.at[at], recv_sem=recv_sem.at[at],
            device_id=device, device_id_type=MESH)

        def where(cond, act):
            if cond is None:
                act()
            else:
                pl.when(cond)(act)

        where(gives, copy.start)
        sent.append(lambda: where(gives, copy.wait_send))
        return lambda: where(takes, copy.wait_recv)

    def leftward(ref):
        return [send(ref.at[:, o:o + n], ref.at[:, h:h + n], linear(-k), me >= k, me + k < nd)
                for h, n, k, o in spans]

    def rightward(ref, dst):
        return [send(ref.at[:, h:h + n], dst.at[:, h - own:h - own + n], linear(k), me + k < nd, me >= k)
                for h, n, k, o in spans]

    def add_received(ref, got):
        for h, n, k, o in spans:
            ref[:, o:o + n] += jnp.where(me >= k, got[:, h - own:h - own + n], 0.0)

    tot1[...] = jnp.zeros_like(tot1)
    tot2[...] = jnp.zeros_like(tot2)
    vb[8:16, :] = jnp.zeros((8, own + 2 * TS), jnp.bfloat16)
    for copy in loads:
        copy.wait()

    mine = c_in[...] * SCALE
    win_c[:, 0:own] = mine
    row_c[...] = jnp.transpose(jnp.concatenate([mine] * 4, axis=0))
    vb[0:8, 0:own] = win_r[:, 0:own].astype(jnp.bfloat16)

    slot = lax.broadcasted_iota(jnp.int32, (1, pairs.shape[1]), 1)
    alive = slot < count[0]
    pi, pj = pairs[0:1, :], pairs[1:2, :]

    def far_flag(o):
        i = me * tiles + o
        hit = (pi == i) & (pj == i + 2) & alive
        return jnp.max(jnp.where(hit, 1.0, 0.0), axis=1, keepdims=True)

    def near_flag(o):
        return jnp.where(me * tiles + o + 1 < nd * tiles, 1.0, 0.0).astype(jnp.float32)

    def fold(value):
        return value[0:8] + value[8:16]

    def contract(tot, o, h, rows, chunk, flag):
        at = pl.multiple_of(o * TS + rows, PIECE)
        here = vb[:, pl.ds(at, PIECE)]
        there = vb[:, h * TS:(h + 1) * TS]
        col = fold(jnp.dot(here, chunk, preferred_element_type=jnp.float32))
        row = fold(lax.dot_general(there, chunk, (((1,), (1,)), ((), ())),
                                   preferred_element_type=jnp.float32))
        if flag is not None:
            col, row = col * flag, row * flag
        tot[:, h * TS:(h + 1) * TS] += col
        tot[:, pl.ds(at, PIECE)] += row

    def cov_chunk(o, h, rows):
        at = pl.multiple_of(o * TS + rows, PIECE)
        xr, yr = row_c[pl.ds(at, PIECE), 0:1], row_c[pl.ds(at, PIECE), 1:2]
        xc, yc = win_c[0:1, h * TS:(h + 1) * TS], win_c[1:2, h * TS:(h + 1) * TS]
        return covariance(xr, yr, xc, yc)

    blocks = [(o, o + 1) for o in range(tiles)] + [(o, o + 2) for o in range(tiles)]
    local = [b for b, (o, h) in enumerate(blocks) if h < tiles]
    cross = [b for b, (o, h) in enumerate(blocks) if h >= tiles]
    flags = {}
    for b, (o, h) in enumerate(blocks):
        if h - o == 2:
            flags[b] = far_flag(o)
        else:
            flags[b] = near_flag(o) if h >= tiles else None

    def full_block(b, tot, build):
        o, h = blocks[b]

        def step(i, carry):
            rows = pl.multiple_of(i * PIECE, PIECE)
            if build:
                chunk = cov_chunk(o, h, rows)
                full_c[b, pl.ds(rows, PIECE), :] = chunk
            else:
                chunk = full_c[b, pl.ds(rows, PIECE), :]
            contract(tot, o, h, rows, chunk, flags[b])
            return carry

        lax.fori_loop(0, STEPS, step, 0)

    def diag_block(o, tot, build):
        for k in range(STEPS):
            for l in range(k, STEPS):
                rk = slice(o * TS + k * PIECE, o * TS + (k + 1) * PIECE)
                rl = slice(o * TS + l * PIECE, o * TS + (l + 1) * PIECE)
                ck, cl = slice(k * PIECE, (k + 1) * PIECE), slice(l * PIECE, (l + 1) * PIECE)
                if build:
                    chunk = covariance(row_c[rk, 0:1], row_c[rk, 1:2], win_c[0:1, rl], win_c[1:2, rl])
                    diag_c[o, ck, cl] = chunk
                else:
                    chunk = diag_c[o, ck, cl]
                tot[:, rl] += fold(jnp.dot(vb[:, rk], chunk, preferred_element_type=jnp.float32))
                if k != l:
                    tot[:, rk] += fold(lax.dot_general(
                        vb[:, rl], chunk, (((1,), (1,)), ((), ())), preferred_element_type=jnp.float32))

    def all_sum(value, at, dst):
        part[at] = value
        if direct:
            waits = [send(part.at[at], dst.at[d - 1], linear(d)) for d in range(1, nd)]
            at_end = at
            first_slot = 0
        else:
            waits = [send(part.at[at], dst.at[d - 1], sub_peer(d)) for d in range(1, ns)]
            for d, wait in enumerate(waits):
                wait()
            total = part[at]
            for d in range(ns - 1):
                total = total + dst[d]
            at_end = at + 1
            part[at_end] = total
            first_slot = ns - 1
            waits = [send(part.at[at_end], dst.at[ns - 1 + d - 1], tile_peer(d)) for d in range(1, nt)]

        def end():
            total = part[at_end]
            for wait in waits:
                wait()
            for d in range(len(waits)):
                total = total + dst[first_slot + d]
            return total

        return end

    for o in range(tiles - 1):
        diag_block(o, tot1, True)
    pl.semaphore_wait(barrier, len(greet))
    waits = leftward(win_c) + leftward(win_r)
    for b in local:
        full_block(b, tot1, True)
    for wait in waits:
        wait()
    vb[0:8, own:] = win_r[:, own:].astype(jnp.bfloat16)
    for b in cross:
        full_block(b, tot1, True)
    waits = rightward(tot1, got1)
    diag_block(tiles - 1, tot1, True)
    for wait in waits:
        wait()

    r0 = win_r[:, 0:own]
    win_q[:, 0:own] = r0 + tot1[:, 0:own]
    add_received(win_q, got1)
    waits = leftward(win_q)
    q0 = win_q[:, 0:own]
    high = q0.astype(jnp.bfloat16)
    vb[0:8, 0:own] = high
    vb[8:16, 0:own] = (q0 - high.astype(jnp.float32)).astype(jnp.bfloat16)

    for o in range(tiles - 1):
        diag_block(o, tot2, False)
    for b in local:
        full_block(b, tot2, False)
    for wait in waits:
        wait()
    far_q = win_q[:, own:]
    high = far_q.astype(jnp.bfloat16)
    vb[0:8, own:] = high
    vb[8:16, own:] = (far_q - high.astype(jnp.float32)).astype(jnp.bfloat16)
    for b in cross:
        full_block(b, tot2, False)
    waits = rightward(tot2, got2)
    diag_block(tiles - 1, tot2, False)

    def along(value):
        return jnp.sum(value, axis=1, keepdims=True)

    r0, q0 = win_r[:, 0:own], win_q[:, 0:own]
    lane = lax.broadcasted_iota(jnp.int32, (8, 128), 1)
    message = jnp.zeros((8, 128), jnp.float32)
    for at, value in enumerate((along(r0 * r0), along(r0 * q0), along(q0 * q0),
                                along(win_r[...] * tot2[...]), along(win_q[...] * tot2[...]))):
        message = jnp.where(lane == at, value, message)
    sums = all_sum(message, 0, gather1)

    for wait in waits:
        wait()
    mid[...] = q0 + tot2[:, 0:own]
    add_received(mid, got2)
    sums = sums()
    rr, rq, qq = sums[:, 0:1], sums[:, 1:2], sums[:, 2:3]
    rp, qp = rq + sums[:, 3:4], qq + sums[:, 4:5]
    alpha = rr / rq
    new = alpha * alpha * qq - rr
    beta = new / rr
    near = 1.0 + beta
    bend = near * near * rq - near * alpha * (rp + qq) + alpha * alpha * qp
    step = new / bend
    r0, q0 = win_r[:, 0:own], win_q[:, 0:own]
    x_out[...] = (alpha + step * near) * r0 - (step * alpha) * q0
    r_out[...] = r0 - (alpha + step * near) * q0 + (step * alpha) * mid[...]
    for wait in sent:
        wait()


def local(nt, ns, observations, coords, pairs, pair_count):
    own = observations.shape[1]
    tiles = own // TS
    window = own + 2 * TS
    f32 = jnp.float32
    peers = nt * ns - 1 if nt * ns <= 16 else ns - 1 + nt - 1
    copies = 10 + peers
    out = jax.ShapeDtypeStruct(observations.shape, f32)
    vmem = pl.BlockSpec(memory_space=pltpu.VMEM)
    return pl.pallas_call(
        functools.partial(kernel, nt, ns, tiles),
        out_shape=(out, out),
        in_specs=[pl.BlockSpec(memory_space=pl.ANY)] * 4,
        out_specs=(vmem, vmem),
        scratch_shapes=[
            pltpu.VMEM((2, own), f32),
            pltpu.VMEM((2, pairs.shape[1]), jnp.int32),
            pltpu.SMEM((1,), jnp.int32),
            pltpu.VMEM((2, window), f32),
            pltpu.VMEM((own, 8), f32),
            pltpu.VMEM((8, window), f32),
            pltpu.VMEM((8, window), f32),
            pltpu.VMEM((16, window), jnp.bfloat16),
            pltpu.VMEM((8, window), f32),
            pltpu.VMEM((8, window), f32),
            pltpu.VMEM((8, 2 * TS), f32),
            pltpu.VMEM((8, 2 * TS), f32),
            pltpu.VMEM((tiles, TS, TS), jnp.bfloat16),
            pltpu.VMEM((2 * tiles, TS, TS), jnp.bfloat16),
            pltpu.VMEM((2, 8, 128), f32),
            pltpu.VMEM((peers, 8, 128), f32),
            pltpu.VMEM((8, own), f32),
            pltpu.SemaphoreType.DMA((4,)),
            pltpu.SemaphoreType.DMA((copies,)),
            pltpu.SemaphoreType.DMA((copies,)),
        ],
        compiler_params=pltpu.CompilerParams(
            collective_id=0, has_side_effects=True, vmem_limit_bytes=48 * 1024 * 1024),
    )(observations, coords, pairs[0].T, pair_count)


def solution(mesh):
    in_specs = (
        P(None, ("region", "tile", "sub")),
        P(None, ("region", "tile")),
        P(("region", "tile"), None, None),
        P(("region", "tile")),
    )
    out_specs = (P(None, ("region", "tile", "sub")), P(None, ("region", "tile", "sub")))
    body = functools.partial(local, mesh.shape["tile"], mesh.shape["sub"])
    return jax.shard_map(body, mesh=mesh, in_specs=in_specs, out_specs=out_specs, check_vma=False)
```

time: 46.8 us -> 42.2 us (0.902)
  Pallas kernels: 41.5 us -> 37 us
    pallas_call x1, Pallas kernels: 41.5 us -> 37 us  [local(): pl.pallas_call(functools.partial(kernel, nt, ns, tiles), out_shape=(out,...]
where the time goes in v2:
time: 42.2 us; the launch traced here: 41.9 us
  Pallas kernels  37 us (88%)
  local copies, waits for them, and re-layouts  3.61 us (9%)
  between operations  1.3 us (3%)
    pallas_call x1, Pallas kernels, local(): pl.pallas_call(functools.partial(kernel, nt, ns, tiles), out_shape=(out,...  37 us
    unnamed x8, local copies, waits for them, and re-layouts  3.61 us

profile of v2, /device:TPU:0, one launch (start us, length us, event | category | flops | bytes accessed | tf_op | source)
XLA Modules:
  0.0 41.9 jit_solution(8251592734878611970)
XLA Ops:
  1.3 0.0 copy-start.2
  1.3 0.7 %copy-done.2 = s32[1,48,2]{1,2,0:T(2,128)S(1)} copy-done((s32[1,48,2]{1,2,0:T(2,128)S(1)}, s32[1,48,2]{1,2,0:T(2,128)}, u32[]{:S(2)}) %copy-start.2) | copy-done | bytes 408
  2.0 0.0 copy-start
  2.0 0.8 %copy-done = f32[8,2048]{1,0:T(8,128)S(1)} copy-done((f32[8,2048]{1,0:T(8,128)S(1)}, f32[8,2048]{1,0:T(8,128)}, u32[]{:S(2)}) %copy-start) | copy-done | bytes 65560
  2.8 0.0 copy-start.1
  2.8 0.8 %copy-done.1 = f32[2,8192]{1,0:T(2,128)S(1)} copy-done((f32[2,8192]{1,0:T(2,128)S(1)}, f32[2,8192]{1,0:T(2,128)}, u32[]{:S(2)}) %copy-start.1) | copy-done | bytes 65560
  3.6 37.0 %shard_map.59 = (f32[8,2048]{1,0:T(8,128)S(1)}, f32[8,2048]{1,0:T(8,128)S(1)}) custom-call(f32[8,2048]{1,0:T(8,128)S(1)} %copy-done, f32[2,8192]{1,0:T(2,128)S(1)} %copy-done.1, s32[2,48]{1,0:T(2,128)S(1)} %bitcast.3, s32[1]{0:T(128)S(6)} %copy.8.count_in), custom_call_target="tpu_custom_call" | custom-call | tf_op jit(solution)/shard_map/pallas_call | solution.py:305
  40.7 0.6 %copy.9 = f32[8,2048]{1,0:T(8,128)} copy(f32[8,2048]{1,0:T(8,128)S(1)} %get-tuple-element.4) | data formatting | bytes 131072
  41.3 0.6 %copy.10 = f32[8,2048]{1,0:T(8,128)} copy(f32[8,2048]{1,0:T(8,128)S(1)} %get-tuple-element.5) | data formatting | bytes 131072
Async XLA Ops:
  1.3 0.7 %copy-start.2 = (s32[1,48,2]{1,2,0:T(2,128)S(1)}, s32[1,48,2]{1,2,0:T(2,128)}, u32[]{:S(2)}) copy-start(s32[1,48,2]{1,2,0:T(2,128)} %param.6) | copy-start | bytes 1156
  2.0 0.8 %copy-start = (f32[8,2048]{1,0:T(8,128)S(1)}, f32[8,2048]{1,0:T(8,128)}, u32[]{:S(2)}) copy-start(f32[8,2048]{1,0:T(8,128)} %obs.1) | copy-start | bytes 196612
  2.8 0.8 %copy-start.1 = (f32[2,8192]{1,0:T(2,128)S(1)}, f32[2,8192]{1,0:T(2,128)}, u32[]{:S(2)}) copy-start(f32[2,8192]{1,0:T(2,128)} %coords.1) | copy-start | bytes 196612

commit v3 on v2

--- a/solution.py
+++ b/solution.py
@@ -135,48 +135,41 @@
     def fold(value):
         return value[0:8] + value[8:16]
 
-    def contract(tot, o, h, rows, chunk, flag):
-        at = pl.multiple_of(o * TS + rows, PIECE)
-        here = vb[:, pl.ds(at, PIECE)]
-        there = vb[:, h * TS:(h + 1) * TS]
-        col = fold(jnp.dot(here, chunk, preferred_element_type=jnp.float32))
-        row = fold(lax.dot_general(there, chunk, (((1,), (1,)), ((), ())),
-                                   preferred_element_type=jnp.float32))
-        if flag is not None:
-            col, row = col * flag, row * flag
-        tot[:, h * TS:(h + 1) * TS] += col
-        tot[:, pl.ds(at, PIECE)] += row
-
-    def cov_chunk(o, h, rows):
-        at = pl.multiple_of(o * TS + rows, PIECE)
-        xr, yr = row_c[pl.ds(at, PIECE), 0:1], row_c[pl.ds(at, PIECE), 1:2]
-        xc, yc = win_c[0:1, h * TS:(h + 1) * TS], win_c[1:2, h * TS:(h + 1) * TS]
-        return covariance(xr, yr, xc, yc)
-
-    blocks = [(o, o + 1) for o in range(tiles)] + [(o, o + 2) for o in range(tiles)]
-    local = [b for b, (o, h) in enumerate(blocks) if h < tiles]
-    cross = [b for b, (o, h) in enumerate(blocks) if h >= tiles]
-    flags = {}
-    for b, (o, h) in enumerate(blocks):
-        if h - o == 2:
-            flags[b] = far_flag(o)
-        else:
-            flags[b] = near_flag(o) if h >= tiles else None
-
-    def full_block(b, tot, build):
-        o, h = blocks[b]
-
-        def step(i, carry):
-            rows = pl.multiple_of(i * PIECE, PIECE)
-            if build:
-                chunk = cov_chunk(o, h, rows)
-                full_c[b, pl.ds(rows, PIECE), :] = chunk
-            else:
-                chunk = full_c[b, pl.ds(rows, PIECE), :]
-            contract(tot, o, h, rows, chunk, flags[b])
+    fars = [far_flag(o) for o in range(tiles)]
+    nears = [near_flag(o) for o in range(tiles)]
+
+    def flag_of(b):
+        value = jnp.zeros((1, 1), jnp.float32)
+        for at, flag in enumerate(nears + fars):
+            value = jnp.where(b == at, flag, value)
+        return value
+
+    def full_blocks(tot, build, arrive):
+        def step(b, carry):
+            pl.when(b == tiles - 1)(arrive)
+            o = lax.rem(b, tiles)
+            h = o + 1 + lax.div(b, tiles)
+            o_at, h_at = pl.multiple_of(o * TS, TS), pl.multiple_of(h * TS, TS)
+            flag = flag_of(b)
+            there = vb[:, pl.ds(h_at, TS)]
+            xc, yc = win_c[0:1, pl.ds(h_at, TS)], win_c[1:2, pl.ds(h_at, TS)]
+            col = jnp.zeros((16, TS), jnp.float32)
+            for i in range(STEPS):
+                rows = slice(i * PIECE, (i + 1) * PIECE)
+                at = pl.multiple_of(o_at + i * PIECE, PIECE)
+                if build:
+                    chunk = covariance(row_c[pl.ds(at, PIECE), 0:1], row_c[pl.ds(at, PIECE), 1:2], xc, yc)
+                    full_c[b, rows, :] = chunk
+                else:
+                    chunk = full_c[b, rows, :]
+                col += jnp.dot(vb[:, pl.ds(at, PIECE)], chunk, preferred_element_type=jnp.float32)
+                row = lax.dot_general(there, chunk, (((1,), (1,)), ((), ())),
+                                      preferred_element_type=jnp.float32)
+                tot[:, pl.ds(at, PIECE)] += fold(row) * flag
+            tot[:, pl.ds(h_at, TS)] += fold(col) * flag
             return carry
 
-        lax.fori_loop(0, STEPS, step, 0)
+        lax.fori_loop(0, 2 * tiles, step, 0)
 
     def diag_block(o, tot, build):
         for k in range(STEPS):
@@ -225,14 +218,14 @@
     for o in range(tiles - 1):
         diag_block(o, tot1, True)
     pl.semaphore_wait(barrier, len(greet))
-    waits = leftward(win_c) + leftward(win_r)
-    for b in local:
-        full_block(b, tot1, True)
-    for wait in waits:
-        wait()
-    vb[0:8, own:] = win_r[:, own:].astype(jnp.bfloat16)
-    for b in cross:
-        full_block(b, tot1, True)
+    waits_r = leftward(win_c) + leftward(win_r)
+
+    def arrive_r():
+        for wait in waits_r:
+            wait()
+        vb[0:8, own:] = win_r[:, own:].astype(jnp.bfloat16)
+
+    full_blocks(tot1, True, arrive_r)
     waits = rightward(tot1, got1)
     diag_block(tiles - 1, tot1, True)
     for wait in waits:
@@ -241,7 +234,7 @@
     r0 = win_r[:, 0:own]
     win_q[:, 0:own] = r0 + tot1[:, 0:own]
     add_received(win_q, got1)
-    waits = leftward(win_q)
+    waits_q = leftward(win_q)
     q0 = win_q[:, 0:own]
     high = q0.astype(jnp.bfloat16)
     vb[0:8, 0:own] = high
@@ -249,16 +242,16 @@
 
     for o in range(tiles - 1):
         diag_block(o, tot2, False)
-    for b in local:
-        full_block(b, tot2, False)
-    for wait in waits:
-        wait()
-    far_q = win_q[:, own:]
-    high = far_q.astype(jnp.bfloat16)
-    vb[0:8, own:] = high
-    vb[8:16, own:] = (far_q - high.astype(jnp.float32)).astype(jnp.bfloat16)
-    for b in cross:
-        full_block(b, tot2, False)
+
+    def arrive_q():
+        for wait in waits_q:
+            wait()
+        far_q = win_q[:, own:]
+        high = far_q.astype(jnp.bfloat16)
+        vb[0:8, own:] = high
+        vb[8:16, own:] = (far_q - high.astype(jnp.float32)).astype(jnp.bfloat16)
+
+    full_blocks(tot2, False, arrive_q)
     waits = rightward(tot2, got2)
     diag_block(tiles - 1, tot2, False)
 

time: 42.2 us -> 37.5 us (0.89)
  Pallas kernels: 37 us -> 32.4 us
    pallas_call x1, Pallas kernels: 37 us -> 32.4 us  [local(): pl.pallas_call(functools.partial(kernel, nt, ns, tiles), out_shape=(out,...]
where the time goes in v3:
time: 37.5 us; the launch traced here: 37.3 us
  Pallas kernels  32.4 us (86%)
  local copies, waits for them, and re-layouts  3.61 us (10%)
  between operations  1.3 us (3%)
    pallas_call x1, Pallas kernels, local(): pl.pallas_call(functools.partial(kernel, nt, ns, tiles), out_shape=(out,...  32.4 us
    unnamed x8, local copies, waits for them, and re-layouts  3.61 us

profile of v3, /device:TPU:0, one launch (start us, length us, event | category | flops | bytes accessed | tf_op | source)
XLA Modules:
  0.0 37.3 jit_solution(17821106231170944928)
XLA Ops:
  1.3 0.0 copy-start.2
  1.3 0.7 %copy-done.2 = s32[1,48,2]{1,2,0:T(2,128)S(1)} copy-done((s32[1,48,2]{1,2,0:T(2,128)S(1)}, s32[1,48,2]{1,2,0:T(2,128)}, u32[]{:S(2)}) %copy-start.2) | copy-done | bytes 408
  2.0 0.0 copy-start
  2.0 0.8 %copy-done = f32[8,2048]{1,0:T(8,128)S(1)} copy-done((f32[8,2048]{1,0:T(8,128)S(1)}, f32[8,2048]{1,0:T(8,128)}, u32[]{:S(2)}) %copy-start) | copy-done | bytes 65560
  2.8 0.0 copy-start.1
  2.8 0.8 %copy-done.1 = f32[2,8192]{1,0:T(2,128)S(1)} copy-done((f32[2,8192]{1,0:T(2,128)S(1)}, f32[2,8192]{1,0:T(2,128)}, u32[]{:S(2)}) %copy-start.1) | copy-done | bytes 65560
  3.6 32.4 %shard_map.59 = (f32[8,2048]{1,0:T(8,128)S(1)}, f32[8,2048]{1,0:T(8,128)S(1)}) custom-call(f32[8,2048]{1,0:T(8,128)S(1)} %copy-done, f32[2,8192]{1,0:T(2,128)S(1)} %copy-done.1, s32[2,48]{1,0:T(2,128)S(1)} %bitcast.3, s32[1]{0:T(128)S(6)} %copy.8.count_in), custom_call_target="tpu_custom_call" | custom-call | tf_op jit(solution)/shard_map/pallas_call | solution.py:298
  36.0 0.6 %copy.9 = f32[8,2048]{1,0:T(8,128)} copy(f32[8,2048]{1,0:T(8,128)S(1)} %get-tuple-element.4) | data formatting | bytes 131072
  36.7 0.6 %copy.10 = f32[8,2048]{1,0:T(8,128)} copy(f32[8,2048]{1,0:T(8,128)S(1)} %get-tuple-element.5) | data formatting | bytes 131072
Async XLA Ops:
  1.3 0.7 %copy-start.2 = (s32[1,48,2]{1,2,0:T(2,128)S(1)}, s32[1,48,2]{1,2,0:T(2,128)}, u32[]{:S(2)}) copy-start(s32[1,48,2]{1,2,0:T(2,128)} %param.6) | copy-start | bytes 1156
  2.0 0.8 %copy-start = (f32[8,2048]{1,0:T(8,128)S(1)}, f32[8,2048]{1,0:T(8,128)}, u32[]{:S(2)}) copy-start(f32[8,2048]{1,0:T(8,128)} %obs.1) | copy-start | bytes 196612
  2.8 0.8 %copy-start.1 = (f32[2,8192]{1,0:T(2,128)S(1)}, f32[2,8192]{1,0:T(2,128)}, u32[]{:S(2)}) copy-start(f32[2,8192]{1,0:T(2,128)} %coords.1) | copy-start | bytes 196612
